TPU v7x, 32 devices: a whole 2x2x4 slice. The times are simulated.
32 devices in a mesh: gx: 4 (over z), yz: 8 (over y, x, core).
Axes of the slice: x: 2, y: 2, z: 4, core: 2. Of those that a mesh axis runs over, the one named last changes fastest.
Arguments:
- features: bfloat16 [384, 96, 512], P(('gx', 'yz')), may hold values from -6 to 6
- occupancy: int32 [384, 512], P(('gx', 'yz')), may hold values 0 or 1
- neighbours: int32 [384, 27], P(('gx', 'yz')), may hold values from 0 to 84, as said below
- exports: int32 [256], P(('gx', 'yz')), may hold values from 0 to 11, as said below
- coarse_map: int32 [384, 2], P(('gx', 'yz')), may hold values from 0 to 7, as said below
- owners: int32 [128], P(('gx', 'yz')), may hold values from 0 to 7, as said below
- w_sub: bfloat16 [27, 96, 96], replicated, may hold values from -0.15625 to 0.15625
- w_down: bfloat16 [8, 192, 96], replicated, may hold values from -0.3125 to 0.3125
- cotangent: bfloat16 [256, 192, 512], P(('gx', 'yz')), may hold values from -6 to 6
Outputs:
- coarse: bfloat16 [256, 192, 512], P(('gx', 'yz'))
- grad_features: bfloat16 [384, 96, 512], P(('gx', 'yz'))
- grad_sub: float32 [27, 96, 96], replicated
- grad_down: float32 [8, 192, 96], replicated
Inputs may be any that keep to these rules, and one draw needn't show every extreme that they name: `neighbours`: entry 13 of a brick is its own slot. Entries follow the geometry of a map of 8-voxel bricks in which device (i, j) holds a region of 4 x 4 x 2 brick cells beside the regions of (i +- 1, j +- 1); a brick met at offset k meets the first at the opposite offset. Entries that point to another device name only bricks on that device's side faces. `exports`: each device's 8 entries are distinct slots of its bricks that lie on its region's side faces, and every such brick is listed. `coarse_map`: column 0 is the coarse cell (0 to 3), column 1 the octant; every coarse cell of every device holds exactly 3 of its fine bricks, in distinct octants. The 4 coarse cells of one device have distinct owners; in every gx slab one owner is named by every device of the slab.
All inputs are finite; a program needn't handle non-finite values. No bound on the sum of `occupancy` on one device may be relied on, other than what follows from the above.
Results may differ from a plain program's by a relative error of at most 0.0062.
Values may be sent and summed in bfloat16 or wider, within the bound.
A program may use at most 320 MiB of HBM per device.

v0:
```python
import jax
import jax.numpy as jnp
from jax import lax
from jax.sharding import PartitionSpec as P

EDGE = 8


def padded_2(x, sides, width):
    for axis, dim in sides:
        size, length = (lax.axis_size(axis), x.shape[dim])
        up = [(i, (i + 1) % size) for i in range(size - 1)]
        down = [(j, i) for i, j in up]
        last = lax.slice_in_dim(x, length - width, length, axis=dim)
        initial = lax.slice_in_dim(x, 0, width, axis=dim)
        before = lax.ppermute(last, axis, up)
        after = lax.ppermute(initial, axis, down)
        x = jnp.concatenate([before, x, after], axis=dim)
    return x


def silu_slope(values):
    sig = jax.nn.sigmoid(values)
    return sig * (1.0 + values * (1.0 - sig))


def layer_span(shift, cube_edge):
    if shift < 0:
        return (slice(cube_edge - 1, cube_edge), slice(0, 1))
    if shift > 0:
        return (slice(0, 1), slice(cube_edge + 1, cube_edge + 2))
    return (slice(0, cube_edge), slice(1, cube_edge + 1))


def pad_bricks(lookup, neighbour_ids, cube_edge):
    channels = lookup.shape[1]
    blocks = lookup.reshape(lookup.shape[0], channels, cube_edge, cube_edge, cube_edge)
    padded = jnp.zeros(
        (neighbour_ids.shape[0], channels, cube_edge + 2, cube_edge + 2, cube_edge + 2),
        lookup.dtype,
    )
    for offset in range(27):
        spans = [
            layer_span(shift, cube_edge)
            for shift in (offset // 9 - 1, offset // 3 % 3 - 1, offset % 3 - 1)
        ]
        facing = blocks[:, :, spans[0][0], spans[1][0], spans[2][0]]
        picked = jnp.take(facing, neighbour_ids[:, offset], axis=0)
        padded = padded.at[:, :, spans[0][1], spans[1][1], spans[2][1]].set(picked)
    return padded


def conv_forward(padded, weights, cube_edge):
    result = None
    for offset in range(27):
        start_x, start_y, start_z = (offset // 9, offset // 3 % 3, offset % 3)
        window = padded[
            :,
            :,
            start_x : start_x + cube_edge,
            start_y : start_y + cube_edge,
            start_z : start_z + cube_edge,
        ]
        term = jnp.einsum(
            "oi,bixyz->boxyz", weights[offset], window, preferred_element_type=jnp.float32
        )
        result = term if result is None else result + term
    return result


def conv_transpose(padded, weights, cube_edge):
    result = None
    for offset in range(27):
        start_x, start_y, start_z = (2 - offset // 9, 2 - offset // 3 % 3, 2 - offset % 3)
        window = padded[
            :,
            :,
            start_x : start_x + cube_edge,
            start_y : start_y + cube_edge,
            start_z : start_z + cube_edge,
        ]
        term = jnp.einsum(
            "oi,boxyz->bixyz", weights[offset], window, preferred_element_type=jnp.float32
        )
        result = term if result is None else result + term
    return result


def conv_weights(padded, grads, cube_edge):
    terms = []
    for offset in range(27):
        start_x, start_y, start_z = (offset // 9, offset // 3 % 3, offset % 3)
        window = padded[
            :,
            :,
            start_x : start_x + cube_edge,
            start_y : start_y + cube_edge,
            start_z : start_z + cube_edge,
        ]
        terms.append(
            jnp.einsum("boxyz,bixyz->oi", grads, window, preferred_element_type=jnp.float32)
        )
    return jnp.stack(terms)


def split_fine(values, half_edge):
    rows, channels = (values.shape[0], values.shape[1])
    shaped = values.reshape(rows, channels, half_edge, 2, half_edge, 2, half_edge, 2)
    return shaped.transpose(0, 1, 3, 5, 7, 2, 4, 6).reshape(rows, channels, 8, half_edge**3)


def join_fine(values, half_edge):
    rows, channels = (values.shape[0], values.shape[1])
    shaped = values.reshape(rows, channels, 2, 2, 2, half_edge, half_edge, half_edge)
    return shaped.transpose(0, 1, 5, 2, 6, 3, 7, 4).reshape(rows, channels, 8 * half_edge**3)


def split_block(values, half_edge):
    rows, channels = (values.shape[0], values.shape[1])
    shaped = values.reshape(rows, channels, 2, half_edge, 2, half_edge, 2, half_edge)
    return shaped.transpose(0, 1, 2, 4, 6, 3, 5, 7).reshape(rows, channels, 8, half_edge**3)


def join_block(values, half_edge):
    rows, channels = (values.shape[0], values.shape[1])
    shaped = values.reshape(rows, channels, 2, 2, 2, half_edge, half_edge, half_edge)
    return shaped.transpose(0, 1, 2, 5, 3, 6, 4, 7).reshape(rows, channels, 8 * half_edge**3)


def rim_lookup(own_bricks, exports, forward):
    voxels = own_bricks.shape[2]
    outgoing = jnp.take(own_bricks, exports, axis=0)
    if forward:
        arrived = padded_2(outgoing[None, None], (("gx", 0), ("yz", 1)), 1)
    else:
        arrived = padded_2(outgoing[None, None], (("gx", 0), ("yz", 1)), 1)
    arrived = arrived.reshape(-1, own_bricks.shape[1], voxels)
    blank = jnp.zeros((1, own_bricks.shape[1], voxels), own_bricks.dtype)
    return jnp.concatenate([own_bricks, arrived, blank], axis=0)


def activate_coarse(coarse_pre, cotangent):
    coarse_wide = coarse_pre.astype(jnp.float32)
    grad_coarse = (cotangent.astype(jnp.float32) * silu_slope(coarse_wide)).astype(jnp.bfloat16)
    return grad_coarse


def on_device(
    features, occupancy, neighbours, exports, coarse_map, owners, w_sub, w_down, cotangent
):
    bricks = features.shape[0]
    channels = features.shape[1]
    voxels = features.shape[2]
    half_edge = EDGE // 2
    groups = lax.axis_size("yz")
    live = occupancy.astype(jnp.float32).reshape(bricks, 1, EDGE, EDGE, EDGE)
    masked = features * occupancy.astype(jnp.bfloat16)[:, None, :]
    padded_input = pad_bricks(rim_lookup(masked, exports, True), neighbours, EDGE)
    pre_sub = conv_forward(padded_input, w_sub, EDGE) * live
    hidden = jax.nn.silu(pre_sub).astype(jnp.bfloat16)
    strided = split_fine(hidden.reshape(bricks, channels, voxels), half_edge)
    piece = jnp.einsum("toi,bitu->bou", w_down, strided, preferred_element_type=jnp.float32).astype(
        jnp.bfloat16
    )
    cell_of = coarse_map[:, 0]
    octant_of = coarse_map[:, 1]
    owner_of = jnp.take(owners, cell_of)
    group_ids = jnp.arange(groups, dtype=jnp.int32)
    octant_ids = jnp.arange(8, dtype=jnp.int32)
    select = (
        (owner_of[None, None, :] == group_ids[:, None, None])
        & (octant_of[None, None, :] == octant_ids[None, :, None])
    ).astype(jnp.bfloat16)
    outgoing = join_block(
        jnp.einsum("gob,bcu->gcou", select, piece, preferred_element_type=jnp.float32).astype(
            jnp.bfloat16
        ),
        half_edge,
    )
    coarse_pre = lax.all_to_all(outgoing, "yz", split_axis=0, concat_axis=0, tiled=True)
    grad_coarse = activate_coarse(coarse_pre, cotangent)
    returned = split_block(
        lax.all_to_all(grad_coarse, "yz", split_axis=0, concat_axis=0, tiled=True), half_edge
    )
    grad_piece = jnp.einsum(
        "gob,gcou->bcu", select, returned, preferred_element_type=jnp.float32
    ).astype(jnp.bfloat16)
    coarse = jax.nn.silu(coarse_pre.astype(jnp.float32)).astype(jnp.bfloat16)
    down_local = jnp.einsum(
        "bou,bitu->toi", grad_piece, strided, preferred_element_type=jnp.float32
    )
    grad_hidden = join_fine(
        jnp.einsum("toi,bou->bitu", w_down, grad_piece, preferred_element_type=jnp.float32),
        half_edge,
    )
    grad_hidden = grad_hidden.reshape(bricks, channels, EDGE, EDGE, EDGE)
    grad_pre = (grad_hidden * silu_slope(pre_sub) * live).astype(jnp.bfloat16)
    padded_grad = pad_bricks(
        rim_lookup(grad_pre.reshape(bricks, channels, voxels), exports, False), neighbours, EDGE
    )
    grad_input = conv_transpose(padded_grad, w_sub, EDGE) * live
    grad_features = grad_input.reshape(bricks, channels, voxels).astype(jnp.bfloat16)
    sub_local = conv_weights(padded_input, grad_pre, EDGE)
    grad_sub, grad_down = lax.psum((sub_local, down_local), ("gx", "yz"))
    return (coarse, grad_features, grad_sub, grad_down)


def solution(mesh):
    in_specs = (
        P(("gx", "yz"), None, None),
        P(("gx", "yz"), None),
        P(("gx", "yz"), None),
        P(("gx", "yz")),
        P(("gx", "yz"), None),
        P(("gx", "yz")),
        P(),
        P(),
        P(("gx", "yz"), None, None),
    )
    out_specs = (P(("gx", "yz"), None, None), P(("gx", "yz"), None, None), P(), P())
    return jax.shard_map(
        on_device, mesh=mesh, in_specs=in_specs, out_specs=out_specs, check_vma=False
    )
```

profile of v0, /device:TPU:0, one launch (start us, length us, event | category | flops | bytes accessed | tf_op | source)
XLA Modules:
  0.0 806.1 jit_solution(12787594770374967149)
XLA Ops:
  13.5 6.5 collective-permute-start
  38.3 3.1 pad_maximum_fusion.2
  42.7 4.5 collective-permute-start.2
  47.9 3.3 copy.305
  66.5 6.2 pad_maximum_fusion
  72.7 12.1 %copy.306 = bf16[3,3,8,96,512]{3,2,1,0,4:T(8,128)(2,1)} copy(bf16[3,3,8,96,512]{4,3,2,1,0:T(8,128)(2,1)} %pad_maximum_fusion) | data formatting | bytes 14155776 | tf_op jit(solution)/shard_map/concatenate | solution.py:18
  84.8 8.6 %maximum_maximum_fusion = bf16[85,96,8,8,8]{1,0,4,3,2:T(8,128)(2,1)S(1)} fusion(bf16[72,96,8,8,8]{1,0,4,3,2:T(8,128)(2,1)} %bitcast.1018, bf16[12,96,8,8,8]{1,0,4,3,2:T(8,128)(2,1)S(1)} %bitcast.1024, bf16[85]{0:T(256)(128)(2,1)S(1)} %copy-done.96), kind=kLoop, calls=%fused_computation.57 | loop fusion | flops 25067520 | bytes 16613546 | tf_op jit(solution)/shard_map/concatenate | solution.py:139
  95.0 6.4 copy.325
  113.5 2.7 scatter.180
  144.0 5.1 gather_fusion.15
  170.6 4.2 fusion.66
  184.3 4.5 fusion.281
  191.4 2.7 fusion.289
  194.2 2.8 fusion.293
  202.3 2.7 fusion.305
  205.1 2.8 fusion.309
  207.9 3.1 fusion.313
  211.0 2.8 fusion.317
  216.5 2.8 fusion.325
  221.9 2.8 fusion.333
  227.3 2.8 fusion.341
  232.8 2.7 fusion.349
  235.5 2.7 fusion.353
  238.2 2.8 fusion.357
  243.8 2.7 fusion.365
  246.5 2.7 fusion.369
  249.2 2.8 fusion.373
  257.4 37.2 %multiply_convert_fusion.1 = (bf16[12,96,8,8,8]{1,0,4,3,2:T(8,128)(2,1)S(1)}, f32[12,96,8,8,8]{1,0,4,3,2:T(8,128)}) fusion(f32[12,8,8,8]{0,3,2,1:T(8,128)S(1)} %bitcast.1029, bf16[12,96,10,10,10]{1,0,4,3,2:T(8,128)(2,1)} %constant_dynamic-update-slice_fusion.7, bf16[27,96,96]{2,1,0:T(8,128)(2,1)} %param.141, f32[12,8,8,8,96]{4,0,3,2,1:T(8,128)} %fusion.281, ...), kind=kOutput, calls=%fused_computation.88 | convolution fusion | flops 132120576 | bytes 116736000 | tf_op jit(solution)/shard_map/oi,bixyz->boxyz/dot_general | solution.py:64
  302.5 2.8 copy.349
  305.3 55.4 %all_to_all.10 = bf16[8,192,512]{2,1,0:T(8,128)(2,1)S(1)} all-to-all(bf16[8,192,512]{2,1,0:T(8,128)(2,1)} %copy.349), channel_id=1, replica_groups=mesh['gx'=4,'yz'=8] {'yz'}, dimensions={0} | all-to-all | bytes 3145728 | tf_op jit(solution)/shard_map/all_to_all | solution.py:180
  360.7 3.2 fusion.10
  363.9 4.3 all-to-all-start.1
  368.2 4.2 copy.395
  372.4 16.8 %all-to-all-done.1 = bf16[8,192,512]{2,1,0:T(8,128)(2,1)} async-done(((bf16[8,192,512]{2,1,0:T(8,128)(2,1)}), bf16[8,192,512]{2,1,0:T(8,128)(2,1)}, u32[]{:S(2)}, u32[]{:S(2)}) %all-to-all-start.1) | async-done | bytes 1572896 | tf_op jit(solution)/shard_map/all_to_all | solution.py:183
  389.2 3.2 copy.350
  392.4 3.5 copy.351
  396.0 3.6 reshape.2536
  407.3 2.9 gather_fusion.29
  413.1 5.0 collective-permute-start.4
  418.1 3.0 fusion.72
  456.2 4.5 collective-permute-start.6
  466.5 132.7 %all-reduce.5.cloned.1.call-done = (f32[27,96,96]{2,1,0:T(8,128)}, f32[8,192,96]{1,0,2:T(8,128)}) async-done(((f32[27,96,96]{2,1,0:T(8,128)}, f32[8,192,96]{1,0,2:T(8,128)}), (f32[27,96,96]{2,1,0:T(8,128)}, f32[8,192,96]{1,0,2:T(8,128)})) %all-reduce.5.cloned.1.call-update) | async-done | bytes 1585168 | tf_op jit(solution)/shard_map/psum | solution.py:204
  601.5 6.2 pad_maximum_fusion.1
  607.8 12.1 %copy.460 = bf16[3,3,8,96,512]{3,2,1,0,4:T(8,128)(2,1)} copy(bf16[3,3,8,96,512]{4,3,2,1,0:T(8,128)(2,1)} %pad_maximum_fusion.1) | data formatting | bytes 14155776 | tf_op jit(solution)/shard_map/concatenate | solution.py:139
  619.8 8.6 %maximum_maximum_fusion.1 = bf16[85,96,8,8,8]{1,0,4,3,2:T(8,128)(2,1)S(1)} fusion(bf16[72,96,8,8,8]{1,0,4,3,2:T(8,128)(2,1)} %bitcast.1017, bf16[12,96,8,8,8]{1,0,4,3,2:T(8,128)(2,1)S(1)} %multiply_convert_fusion, bf16[85]{0:T(256)(128)(2,1)S(1)} %copy-done.97), kind=kLoop, calls=%fused_computation.58 | loop fusion | flops 25067520 | bytes 16613546 | tf_op jit(solution)/shard_map/concatenate | solution.py:139
  634.5 6.3 copy.375
  666.3 5.1 gather_fusion.43
  671.5 2.8 copy.381
  676.4 2.8 copy.369
  687.4 3.1 fusion.279
  690.5 2.7 fusion.283
  693.2 2.8 fusion.287
  701.3 2.7 fusion.299
  704.0 2.8 fusion.303
  709.4 3.0 fusion.311
  715.2 2.8 fusion.319
  720.6 2.7 fusion.327
  726.0 2.8 fusion.335
  731.4 2.7 fusion.343
  736.8 2.8 fusion.351
  742.3 2.7 fusion.359
  745.0 2.7 fusion.363
  747.7 2.8 fusion.367
  758.6 35.2 %fusion.1 = bf16[12,96,8,8,8]{1,0,4,3,2:T(8,128)(2,1)S(1)} fusion(f32[12,8,8,8,96]{4,0,3,2,1:T(8,128)} %fusion.279, f32[12,8,8,8,96]{4,0,3,2,1:T(8,128)} %fusion.283, f32[12,8,8,8,96]{4,0,3,2,1:T(8,128)} %fusion.287, f32[12,8,8,8,96]{4,0,3,2,1:T(8,128)} %fusion.291, f32[12,8,8,8,96]{4,0,3,2,1:T(8,128)} %fusion.295, f32[12,8,8,8,96]{4,0,3,2,1:T(8,128)} %fusion.299, ...), kind=kOutput, calls=%fused_computation.66 | convolution fusion | flops 129761280 | bytes 114376704 | tf_op jit(solution)/shard_map/oi,boxyz->bixyz/dot_general | solution.py:82
  (507 shorter events, 280.5 us)
Async XLA Ops:
  7.2 289.4 %copy-start = (bf16[8,192,96]{2,1,0:T(8,128)(2,1)S(1)}, bf16[8,192,96]{2,1,0:T(8,128)(2,1)}, u32[]{:S(2)}) copy-start(bf16[8,192,96]{2,1,0:T(8,128)(2,1)} %param.142) | copy-start | bytes 884740
  7.2 12.8 %copy-start.11 = (s32[12,27]{1,0:T(8,128)S(1)}, s32[12,27]{1,0:T(8,128)}, u32[]{:S(2)}) copy-start(s32[12,27]{1,0:T(8,128)} %param.137) | copy-start | bytes 3892
  7.2 13.6 %copy-start.95 = (s32[12,2]{0,1:T(2,128)S(1)}, s32[12,2]{0,1:T(2,128)}, u32[]{:S(2)}) copy-start(s32[12,2]{0,1:T(2,128)} %param.139) | copy-start | bytes 292
  7.2 15.0 %copy-start.5 = (s32[4]{0:T(128)S(1)}, s32[4]{0:T(128)}, u32[]{:S(2)}) copy-start(s32[4]{0:T(128)} %param.140) | copy-start | bytes 52
  7.9 33.5 %copy-start.98 = (pred[8]{0:T(512)(128)(4,1)}, pred[8]{0:T(512)(128)(4,1)S(1)}, u32[]{:S(2)}) copy-start(pred[8]{0:T(512)(128)(4,1)S(1)} %compare_and_fusion.27) | copy-start | bytes 28
  8.6 32.8 %copy-start.33 = (s32[1024]{0:T(1024)}, s32[1024]{0:T(1024)S(1)}, u32[]{:S(2)}) copy-start(s32[1024]{0:T(1024)S(1)} %pad_clamp_fusion.28) | copy-start | bytes 12292
  11.4 30.0 %copy-start.8 = (bf16[12,96,512]{2,1,0:T(8,128)(2,1)}, bf16[12,96,512]{2,1,0:T(8,128)(2,1)S(1)}, u32[]{:S(2)}) copy-start(bf16[12,96,512]{2,1,0:T(8,128)(2,1)S(1)} %broadcast_multiply_fusion) | copy-start | bytes 3538948
  12.2 26.1 %collective-permute-start.1 = (bf16[1,1,8,96,512]{4,3,2,1,0:T(8,128)(2,1)S(1)}, bf16[1,1,8,96,512]{4,3,2,1,0:T(8,128)(2,1)S(1)}, u32[]{:S(2)}, u32[]{:S(2)}) collective-permute-start(bf16[1,1,8,96,512]{4,3,2,1,0:T(8,128)(2,1)S(1)} %select_bitcast_fusion.1), channel_id=1, source_target_pairs={{8,0},{16,8},{24,16},{9,1},{17,9},{25,17},{10,2},{18,10},{26,18},{... | collective-permute-start | bytes 2359304 | tf_op jit(solution)/shard_map/ppermute | solution.py:17
  13.5 24.8 %collective-permute-start = (bf16[1,1,8,96,512]{4,3,2,1,0:T(8,128)(2,1)S(1)}, bf16[1,1,8,96,512]{4,3,2,1,0:T(8,128)(2,1)}, u32[]{:S(2)}, u32[]{:S(2)}) collective-permute-start(bf16[1,1,8,96,512]{4,3,2,1,0:T(8,128)(2,1)S(1)} %select_bitcast_fusion.1), channel_id=1, source_target_pairs={{0,8},{8,16},{16,24},{1,9},{9,17},{17,25},{2,10},{10,18},{18,26},{... | collective-permute-start | bytes 2359304 | tf_op jit(solution)/shard_map/ppermute | solution.py:16
  20.3 26.9 %copy-start.52 = (s32[12]{0:T(128)}, s32[12]{0:T(128)S(1)}, u32[]{:S(2)}) copy-start(s32[12]{0:T(128)S(1)} %get-tuple-element.700) | copy-start | bytes 148
  20.3 26.9 %copy-start.70 = (s32[12]{0:T(128)}, s32[12]{0:T(128)S(1)}, u32[]{:S(2)}) copy-start(s32[12]{0:T(128)S(1)} %get-tuple-element.699) | copy-start | bytes 148
  20.8 9.8 %copy-start.64 = (s32[12]{0:T(128)}, s32[12]{0:T(128)S(1)}, u32[]{:S(2)}) copy-start(s32[12]{0:T(128)S(1)} %get-tuple-element.686) | copy-start | bytes 148
  20.8 26.3 %copy-start.53 = (s32[12]{0:T(128)}, s32[12]{0:T(128)S(1)}, u32[]{:S(2)}) copy-start(s32[12]{0:T(128)S(1)} %get-tuple-element.698) | copy-start | bytes 148
  20.9 26.3 %copy-start.54 = (s32[12]{0:T(128)}, s32[12]{0:T(128)S(1)}, u32[]{:S(2)}) copy-start(s32[12]{0:T(128)S(1)} %get-tuple-element.696) | copy-start | bytes 148
  20.9 26.3 %copy-start.55 = (s32[12]{0:T(128)}, s32[12]{0:T(128)S(1)}, u32[]{:S(2)}) copy-start(s32[12]{0:T(128)S(1)} %get-tuple-element.697) | copy-start | bytes 148
  20.9 26.3 %copy-start.56 = (s32[12]{0:T(128)}, s32[12]{0:T(128)S(1)}, u32[]{:S(2)}) copy-start(s32[12]{0:T(128)S(1)} %get-tuple-element.694) | copy-start | bytes 148
  20.9 26.3 %copy-start.57 = (s32[12]{0:T(128)}, s32[12]{0:T(128)S(1)}, u32[]{:S(2)}) copy-start(s32[12]{0:T(128)S(1)} %get-tuple-element.695) | copy-start | bytes 148
  20.9 26.3 %copy-start.58 = (s32[12]{0:T(128)}, s32[12]{0:T(128)S(1)}, u32[]{:S(2)}) copy-start(s32[12]{0:T(128)S(1)} %get-tuple-element.692) | copy-start | bytes 148
  20.9 26.3 %copy-start.59 = (s32[12]{0:T(128)}, s32[12]{0:T(128)S(1)}, u32[]{:S(2)}) copy-start(s32[12]{0:T(128)S(1)} %get-tuple-element.693) | copy-start | bytes 148
  20.9 26.3 %copy-start.60 = (s32[12]{0:T(128)}, s32[12]{0:T(128)S(1)}, u32[]{:S(2)}) copy-start(s32[12]{0:T(128)S(1)} %get-tuple-element.690) | copy-start | bytes 148
  20.9 26.3 %copy-start.61 = (s32[12]{0:T(128)}, s32[12]{0:T(128)S(1)}, u32[]{:S(2)}) copy-start(s32[12]{0:T(128)S(1)} %get-tuple-element.691) | copy-start | bytes 148
  20.9 26.3 %copy-start.62 = (s32[12]{0:T(128)}, s32[12]{0:T(128)S(1)}, u32[]{:S(2)}) copy-start(s32[12]{0:T(128)S(1)} %get-tuple-element.688) | copy-start | bytes 148
  20.9 26.3 %copy-start.63 = (s32[12]{0:T(128)}, s32[12]{0:T(128)S(1)}, u32[]{:S(2)}) copy-start(s32[12]{0:T(128)S(1)} %get-tuple-element.689) | copy-start | bytes 148
  21.0 26.3 %copy-start.66 = (s32[12]{0:T(128)}, s32[12]{0:T(128)S(1)}, u32[]{:S(2)}) copy-start(s32[12]{0:T(128)S(1)} %get-tuple-element.684) | copy-start | bytes 148
  21.0 26.3 %copy-start.67 = (s32[12]{0:T(128)}, s32[12]{0:T(128)S(1)}, u32[]{:S(2)}) copy-start(s32[12]{0:T(128)S(1)} %get-tuple-element.685) | copy-start | bytes 148
  21.0 26.3 %copy-start.68 = (s32[12]{0:T(128)}, s32[12]{0:T(128)S(1)}, u32[]{:S(2)}) copy-start(s32[12]{0:T(128)S(1)} %get-tuple-element.682) | copy-start | bytes 148
  21.0 26.3 %copy-start.69 = (s32[12]{0:T(128)}, s32[12]{0:T(128)S(1)}, u32[]{:S(2)}) copy-start(s32[12]{0:T(128)S(1)} %get-tuple-element.683) | copy-start | bytes 148
  21.0 26.3 %copy-start.71 = (s32[12]{0:T(128)}, s32[12]{0:T(128)S(1)}, u32[]{:S(2)}) copy-start(s32[12]{0:T(128)S(1)} %get-tuple-element.681) | copy-start | bytes 148
  25.2 87.7 %copy-start.29 = (s32[1024]{0:T(1024)}, s32[1024]{0:T(1024)S(1)}, u32[]{:S(2)}) copy-start(s32[1024]{0:T(1024)S(1)} %pad_clamp_fusion.27) | copy-start | bytes 12292
  30.0 88.1 %copy-start.30 = (s32[1024]{0:T(1024)}, s32[1024]{0:T(1024)S(1)}, u32[]{:S(2)}) copy-start(s32[1024]{0:T(1024)S(1)} %pad_clamp_fusion.9) | copy-start | bytes 12292
  30.0 87.5 %copy-start.31 = (s32[1024]{0:T(1024)}, s32[1024]{0:T(1024)S(1)}, u32[]{:S(2)}) copy-start(s32[1024]{0:T(1024)S(1)} %pad_clamp_fusion.7) | copy-start | bytes 12292
  30.7 86.2 %copy-start.32 = (s32[1024]{0:T(1024)}, s32[1024]{0:T(1024)S(1)}, u32[]{:S(2)}) copy-start(s32[1024]{0:T(1024)S(1)} %pad_clamp_fusion.3) | copy-start | bytes 12292
  41.4 25.0 %collective-permute-start.3 = (bf16[3,1,8,96,512]{4,3,2,1,0:T(8,128)(2,1)}, bf16[3,1,8,96,512]{4,3,2,1,0:T(8,128)(2,1)}, u32[]{:S(2)}, u32[]{:S(2)}) collective-permute-start(bf16[3,1,8,96,512]{4,3,2,1,0:T(8,128)(2,1)} %pad_maximum_fusion.2), channel_id=1, source_target_pairs={{1,0},{2,1},{3,2},{4,3},{5,4},{6,5},{7,6},{9,8},{10,9},{11,10},{12... | collective-permute-start | bytes 7077896 | tf_op jit(solution)/shard_map/ppermute | solution.py:17
  42.7 23.7 %collective-permute-start.2 = (bf16[3,1,8,96,512]{4,3,2,1,0:T(8,128)(2,1)}, bf16[3,1,8,96,512]{4,3,2,1,0:T(8,128)(2,1)}, u32[]{:S(2)}, u32[]{:S(2)}) collective-permute-start(bf16[3,1,8,96,512]{4,3,2,1,0:T(8,128)(2,1)} %pad_maximum_fusion.2), channel_id=1, source_target_pairs={{0,1},{1,2},{2,3},{3,4},{4,5},{5,6},{6,7},{8,9},{9,10},{10,11},{11... | collective-permute-start | bytes 7077896 | tf_op jit(solution)/shard_map/ppermute | solution.py:16
  52.1 350.5 %copy-start.12 = (f32[12,512]{0,1:T(8,128)}, f32[12,512]{0,1:T(8,128)S(1)}, u32[]{:S(2)}) copy-start(f32[12,512]{0,1:T(8,128)S(1)} %copy.457) | copy-start | bytes 73732
  72.7 12.1 %copy-start.96 = (bf16[85]{0:T(256)(128)(2,1)S(1)}, bf16[85]{0:T(256)(128)(2,1)}, u32[]{:S(2)}) copy-start(bf16[85]{0:T(256)(128)(2,1)} %pad.231.clone) | copy-start | bytes 514
  153.3 21.5 %copy-start.88 = (pred[12]{0:T(512)(128)(4,1)S(1)}, pred[12]{0:T(512)(128)(4,1)}, u32[]{:S(2)}) copy-start(pred[12]{0:T(512)(128)(4,1)} %get-tuple-element.810) | copy-start | bytes 40
  153.3 22.3 %copy-start.14 = (bf16[12,96,8]{1,2,0:T(8,128)(2,1)S(1)}, bf16[12,96,8]{1,2,0:T(8,128)(2,1)}, u32[]{:S(2)}) copy-start(bf16[12,96,8]{1,2,0:T(8,128)(2,1)} %gather_fusion.17) | copy-start | bytes 55300
  153.3 22.3 %copy-start.47 = (pred[12]{0:T(512)(128)(4,1)S(1)}, pred[12]{0:T(512)(128)(4,1)}, u32[]{:S(2)}) copy-start(pred[12]{0:T(512)(128)(4,1)} %get-tuple-element.809) | copy-start | bytes 40
  153.3 23.0 %copy-start.86 = (pred[12]{0:T(512)(128)(4,1)S(1)}, pred[12]{0:T(512)(128)(4,1)}, u32[]{:S(2)}) copy-start(pred[12]{0:T(512)(128)(4,1)} %get-tuple-element.808) | copy-start | bytes 40
  153.3 23.9 %copy-start.44 = (pred[12]{0:T(512)(128)(4,1)S(1)}, pred[12]{0:T(512)(128)(4,1)}, u32[]{:S(2)}) copy-start(pred[12]{0:T(512)(128)(4,1)} %get-tuple-element.807) | copy-start | bytes 40
  153.4 24.5 %copy-start.79 = (pred[12]{0:T(512)(128)(4,1)S(1)}, pred[12]{0:T(512)(128)(4,1)}, u32[]{:S(2)}) copy-start(pred[12]{0:T(512)(128)(4,1)} %get-tuple-element.806) | copy-start | bytes 40
  153.4 25.2 %copy-start.41 = (pred[12]{0:T(512)(128)(4,1)S(1)}, pred[12]{0:T(512)(128)(4,1)}, u32[]{:S(2)}) copy-start(pred[12]{0:T(512)(128)(4,1)} %get-tuple-element.805) | copy-start | bytes 40
  153.4 25.9 %copy-start.77 = (pred[12]{0:T(512)(128)(4,1)S(1)}, pred[12]{0:T(512)(128)(4,1)}, u32[]{:S(2)}) copy-start(pred[12]{0:T(512)(128)(4,1)} %get-tuple-element.804) | copy-start | bytes 40
  153.4 26.5 %copy-start.38 = (pred[12]{0:T(512)(128)(4,1)S(1)}, pred[12]{0:T(512)(128)(4,1)}, u32[]{:S(2)}) copy-start(pred[12]{0:T(512)(128)(4,1)} %get-tuple-element.803) | copy-start | bytes 40
  153.4 27.3 %copy-start.83 = (pred[12]{0:T(512)(128)(4,1)S(1)}, pred[12]{0:T(512)(128)(4,1)}, u32[]{:S(2)}) copy-start(pred[12]{0:T(512)(128)(4,1)} %get-tuple-element.802) | copy-start | bytes 40
  153.4 28.1 %copy-start.36 = (pred[12]{0:T(512)(128)(4,1)S(1)}, pred[12]{0:T(512)(128)(4,1)}, u32[]{:S(2)}) copy-start(pred[12]{0:T(512)(128)(4,1)} %get-tuple-element.801) | copy-start | bytes 40
  153.4 28.8 %copy-start.74 = (pred[12]{0:T(512)(128)(4,1)S(1)}, pred[12]{0:T(512)(128)(4,1)}, u32[]{:S(2)}) copy-start(pred[12]{0:T(512)(128)(4,1)} %get-tuple-element.800) | copy-start | bytes 40
  153.4 29.5 %copy-start.34 = (pred[12]{0:T(512)(128)(4,1)S(1)}, pred[12]{0:T(512)(128)(4,1)}, u32[]{:S(2)}) copy-start(pred[12]{0:T(512)(128)(4,1)} %get-tuple-element.799) | copy-start | bytes 40
  153.4 30.2 %copy-start.72 = (pred[12]{0:T(512)(128)(4,1)S(1)}, pred[12]{0:T(512)(128)(4,1)}, u32[]{:S(2)}) copy-start(pred[12]{0:T(512)(128)(4,1)} %get-tuple-element.798) | copy-start | bytes 40
  153.4 30.8 %copy-start.18 = (bf16[27,96,96]{2,1,0:T(8,128)(2,1)S(1)}, bf16[27,96,96]{2,1,0:T(8,128)(2,1)}, u32[]{:S(2)}) copy-start(bf16[27,96,96]{2,1,0:T(8,128)(2,1)} %param.141) | copy-start | bytes 1492996
  305.3 55.4 %copy-start.23 = (bf16[8,192,512]{2,1,0:T(8,128)(2,1)S(1)}, bf16[8,192,512]{2,1,0:T(8,128)(2,1)}, u32[]{:S(2)}) copy-start(bf16[8,192,512]{2,1,0:T(8,128)(2,1)} %param.143) | copy-start | bytes 4718596
  363.9 25.4 %all-to-all-start.1 = ((bf16[8,192,512]{2,1,0:T(8,128)(2,1)}), bf16[8,192,512]{2,1,0:T(8,128)(2,1)}, u32[]{:S(2)}, u32[]{:S(2)}) async-start(bf16[8,192,512]{2,1,0:T(8,128)(2,1)} %get-tuple-element.762), calls=%async_computation.1 | async-start | bytes 3145728 | tf_op jit(solution)/shard_map/all_to_all | solution.py:183
  368.2 231.0 %all-reduce.5.cloned.1.call-start = ((), (), s32[]{:S(2)}) async-start(), calls=%async_computation.2 | async-start | bytes 4227072 | tf_op jit(solution)/shard_map/psum | solution.py:204
  411.5 9.5 %copy-start.3 = (bf16[12,96,10,10,10]{1,0,4,3,2:T(8,128)(2,1)S(1)}, bf16[12,96,10,10,10]{1,0,4,3,2:T(8,128)(2,1)}, u32[]{:S(2)}) copy-start(bf16[12,96,10,10,10]{1,0,4,3,2:T(8,128)(2,1)} %constant_dynamic-update-slice_fusion.7) | copy-start | bytes 6912004
  411.5 41.6 %collective-permute-start.5 = (bf16[1,1,8,96,512]{4,3,2,1,0:T(8,128)(2,1)S(1)}, bf16[1,1,8,96,512]{4,3,2,1,0:T(8,128)(2,1)S(1)}, u32[]{:S(2)}, u32[]{:S(2)}) collective-permute-start(bf16[1,1,8,96,512]{4,3,2,1,0:T(8,128)(2,1)S(1)} %select_bitcast_fusion), channel_id=1, source_target_pairs={{8,0},{16,8},{24,16},{9,1},{17,9},{25,17},{10,2},{18,10},{26,18},{... | collective-permute-start | bytes 2359304 | tf_op jit(solution)/shard_map/ppermute | solution.py:17
  413.1 40.0 %collective-permute-start.4 = (bf16[1,1,8,96,512]{4,3,2,1,0:T(8,128)(2,1)S(1)}, bf16[1,1,8,96,512]{4,3,2,1,0:T(8,128)(2,1)S(1)}, u32[]{:S(2)}, u32[]{:S(2)}) collective-permute-start(bf16[1,1,8,96,512]{4,3,2,1,0:T(8,128)(2,1)S(1)} %select_bitcast_fusion), channel_id=1, source_target_pairs={{0,8},{8,16},{16,24},{1,9},{9,17},{17,25},{2,10},{10,18},{18,26},{... | collective-permute-start | bytes 2359304 | tf_op jit(solution)/shard_map/ppermute | solution.py:16
  453.0 9.3 %copy-start.16 = (bf16[1,1,8,96,512]{4,3,2,1,0:T(8,128)(2,1)}, bf16[1,1,8,96,512]{4,3,2,1,0:T(8,128)(2,1)S(1)}, u32[]{:S(2)}) copy-start(bf16[1,1,8,96,512]{4,3,2,1,0:T(8,128)(2,1)S(1)} %collective-permute-done.5) | copy-start | bytes 2359300
  453.1 9.3 %copy-start.17 = (bf16[1,1,8,96,512]{4,3,2,1,0:T(8,128)(2,1)}, bf16[1,1,8,96,512]{4,3,2,1,0:T(8,128)(2,1)S(1)}, u32[]{:S(2)}) copy-start(bf16[1,1,8,96,512]{4,3,2,1,0:T(8,128)(2,1)S(1)} %collective-permute-done.4) | copy-start | bytes 2359300
  454.8 146.7 %collective-permute-start.7 = (bf16[3,1,8,96,512]{4,3,2,1,0:T(8,128)(2,1)}, bf16[3,1,8,96,512]{4,3,2,1,0:T(8,128)(2,1)}, u32[]{:S(2)}, u32[]{:S(2)}) collective-permute-start(bf16[3,1,8,96,512]{4,3,2,1,0:T(8,128)(2,1)} %pad_maximum_fusion.3), channel_id=1, source_target_pairs={{1,0},{2,1},{3,2},{4,3},{5,4},{6,5},{7,6},{9,8},{10,9},{11,10},{12... | collective-permute-start | bytes 7077896 | tf_op jit(solution)/shard_map/ppermute | solution.py:17
  456.2 145.3 %collective-permute-start.6 = (bf16[3,1,8,96,512]{4,3,2,1,0:T(8,128)(2,1)}, bf16[3,1,8,96,512]{4,3,2,1,0:T(8,128)(2,1)}, u32[]{:S(2)}, u32[]{:S(2)}) collective-permute-start(bf16[3,1,8,96,512]{4,3,2,1,0:T(8,128)(2,1)} %pad_maximum_fusion.3), channel_id=1, source_target_pairs={{0,1},{1,2},{2,3},{3,4},{4,5},{5,6},{6,7},{8,9},{9,10},{10,11},{11... | collective-permute-start | bytes 7077896 | tf_op jit(solution)/shard_map/ppermute | solution.py:16
  607.8 12.1 %copy-start.97 = (bf16[85]{0:T(256)(128)(2,1)S(1)}, bf16[85]{0:T(256)(128)(2,1)}, u32[]{:S(2)}) copy-start(bf16[85]{0:T(256)(128)(2,1)} %pad.231.clone) | copy-start | bytes 514
  687.4 68.5 %copy-start.4 = (bf16[12,96,10,10,10]{1,0,4,3,2:T(8,128)(2,1)}, bf16[12,96,10,10,10]{1,0,4,3,2:T(8,128)(2,1)S(1)}, u32[]{:S(2)}) copy-start(bf16[12,96,10,10,10]{1,0,4,3,2:T(8,128)(2,1)S(1)} %constant_dynamic-update-slice_fusion) | copy-start | bytes 6912004
  758.6 40.2 %copy-start.1 = (bf16[8,192,96]{2,1,0:T(8,128)(2,1)S(1)}, bf16[8,192,96]{2,1,0:T(8,128)(2,1)}, u32[]{:S(2)}) copy-start(bf16[8,192,96]{2,1,0:T(8,128)(2,1)} %param.142) | copy-start | bytes 884740
  (48 other events, 218.5 us)
Sparse Core Ops, SparseCore 0:
  466.7 132.4 all-reduce.4
where the time goes:
time: 815 us; the launch traced here: 806 us
  matrix products  260 us (32%)
  local copies, waits for them, and re-layouts  183 us (22%)
  waiting for transfers between devices  149 us (18%)
  other arithmetic  112 us (14%)
  blocking collectives  55.4 us (7%)
  starting transfers between devices  30.3 us (4%)
  between operations  16.4 us (2%)
    psum x1, waiting for transfers between devices, on_device(): grad_sub, grad_down = lax.psum((sub_local, down_local), ('gx', 'yz'))  133 us
    dot_general x27, matrix products, conv_forward(): jnp.einsum('oi,bixyz->boxyz', weights[offset], window, preferred_element_...  110 us
    dot_general x27, matrix products, conv_transpose(): jnp.einsum('oi,boxyz->bixyz', weights[offset], window, preferred_element_...  106 us
    gather x54, local copies, waits for them, and re-layouts, pad_bricks(): picked = jnp.take(facing, neighbour_ids[:, offset], axis=0)  63.4 us
    all_to_all x1, blocking collectives, on_device(): lax.all_to_all(outgoing, 'yz', split_axis=0, concat_axis=0, tiled=True)  55.4 us
    dot_general x27, matrix products, conv_weights(): jnp.einsum('boxyz,bixyz->oi', grads, window, preferred_element_type=jnp.f...  39.1 us
    scatter x52, other arithmetic, pad_bricks(): padded = padded.at[:, :, spans[0][1], spans[1][1], spans[2][1]].set(picked)  35.7 us
    another operation x50, local copies, waits for them, and re-layouts, pad_bricks(): picked = jnp.take(facing, neighbour_ids[:, offset], axis=0)  33.3 us
  transfers between devices with their start and end apart: 10, of which 2 were waited for; matrix products, arithmetic and copies ran while one was open for 10% of the time, Pallas kernels for 0%

commit v1 on v0

--- a/solution.py
+++ b/solution.py
@@ -2,6 +2,7 @@
 import jax.numpy as jnp
 from jax import lax
 from jax.sharding import PartitionSpec as P
+from jax.lax import psum
 
 EDGE = 8
 
@@ -201,7 +202,8 @@
     grad_input = conv_transpose(padded_grad, w_sub, EDGE) * live
     grad_features = grad_input.reshape(bricks, channels, voxels).astype(jnp.bfloat16)
     sub_local = conv_weights(padded_input, grad_pre, EDGE)
-    grad_sub, grad_down = lax.psum((sub_local, down_local), ("gx", "yz"))
+    switch_numbers = lambda page, which_axis, device_axis: psum(psum(page, which_axis), device_axis)
+    grad_sub, grad_down = switch_numbers((sub_local, down_local), "yz", "gx")
     return (coarse, grad_features, grad_sub, grad_down)
 
 

time: 815 us -> 845 us (1.037)
  waiting for transfers between devices: 149 us -> 177 us
    psum x1 -> x2, waiting for transfers between devices: 133 us -> 160 us  [the longest x1 90.7 us: on_device(): psum(psum(page, which_axis), device_axis)]
  transfers between devices with their start and end apart: 10 -> 11, of which waited for: 2 -> 3; matrix products, arithmetic and copies ran while one was open for 10% -> 10% of each run, Pallas kernels for 0% -> 0%
where the time goes in v1:
time: 845 us; the launch traced here: 836 us
  matrix products  260 us (31%)
  local copies, waits for them, and re-layouts  184 us (22%)
  waiting for transfers between devices  177 us (21%)
  other arithmetic  113 us (13%)
  blocking collectives  55.4 us (7%)
  starting transfers between devices  31.1 us (4%)
  between operations  16.4 us (2%)
    dot_general x27, matrix products, conv_forward(): jnp.einsum('oi,bixyz->boxyz', weights[offset], window, preferred_element_...  110 us
    dot_general x27, matrix products, conv_transpose(): jnp.einsum('oi,boxyz->bixyz', weights[offset], window, preferred_element_...  106 us
    psum x1, waiting for transfers between devices, on_device(): psum(psum(page, which_axis), device_axis)  90.7 us
    psum x1, waiting for transfers between devices, on_device(): psum(page, which_axis)  69.4 us
    gather x54, local copies, waits for them, and re-layouts, pad_bricks(): picked = jnp.take(facing, neighbour_ids[:, offset], axis=0)  63.4 us
    all_to_all x1, blocking collectives, on_device(): lax.all_to_all(outgoing, 'yz', split_axis=0, concat_axis=0, tiled=True)  55.4 us
    dot_general x27, matrix products, conv_weights(): jnp.einsum('boxyz,bixyz->oi', grads, window, preferred_element_type=jnp.f...  39 us
    scatter x52, other arithmetic, pad_bricks(): padded = padded.at[:, :, spans[0][1], spans[1][1], spans[2][1]].set(picked)  35.7 us
  transfers between devices with their start and end apart: 11, of which 3 were waited for; matrix products, arithmetic and copies ran while one was open for 10% of the time, Pallas kernels for 0%

profile of v1, /device:TPU:0, one launch (start us, length us, event | category | flops | bytes accessed | tf_op | source)
XLA Modules:
  0.0 836.0 jit_solution(5754169163693725641)
XLA Ops:
  13.5 6.5 collective-permute-start
  38.3 3.1 pad_maximum_fusion.2
  42.7 4.5 collective-permute-start.2
  47.9 3.3 copy.305
  66.5 6.2 pad_maximum_fusion
  72.7 12.1 %copy.306 = bf16[3,3,8,96,512]{3,2,1,0,4:T(8,128)(2,1)} copy(bf16[3,3,8,96,512]{4,3,2,1,0:T(8,128)(2,1)} %pad_maximum_fusion) | data formatting | bytes 14155776 | tf_op jit(solution)/shard_map/concatenate | solution.py:19
  84.8 8.6 %maximum_maximum_fusion = bf16[85,96,8,8,8]{1,0,4,3,2:T(8,128)(2,1)S(1)} fusion(bf16[72,96,8,8,8]{1,0,4,3,2:T(8,128)(2,1)} %bitcast.1018, bf16[12,96,8,8,8]{1,0,4,3,2:T(8,128)(2,1)S(1)} %bitcast.1024, bf16[85]{0:T(256)(128)(2,1)S(1)} %copy-done.94), kind=kLoop, calls=%fused_computation.57 | loop fusion | flops 25067520 | bytes 16613546 | tf_op jit(solution)/shard_map/concatenate | solution.py:140
  95.0 6.4 copy.325
  113.5 2.7 scatter.180
  144.0 5.1 gather_fusion.15
  170.6 4.2 fusion.66
  184.3 4.5 fusion.281
  191.4 2.7 fusion.289
  194.2 2.8 fusion.293
  202.3 2.7 fusion.305
  205.1 2.8 fusion.309
  207.9 3.1 fusion.313
  211.0 2.8 fusion.317
  216.5 2.8 fusion.325
  221.9 2.8 fusion.333
  227.3 2.8 fusion.341
  232.8 2.7 fusion.349
  235.5 2.7 fusion.353
  238.2 2.8 fusion.357
  243.8 2.7 fusion.365
  246.5 2.7 fusion.369
  249.2 2.8 fusion.373
  257.4 37.2 %multiply_convert_fusion.1 = (bf16[12,96,8,8,8]{1,0,4,3,2:T(8,128)(2,1)S(1)}, f32[12,96,8,8,8]{1,0,4,3,2:T(8,128)}) fusion(f32[12,8,8,8]{0,3,2,1:T(8,128)S(1)} %bitcast.1029, bf16[12,96,10,10,10]{1,0,4,3,2:T(8,128)(2,1)} %constant_dynamic-update-slice_fusion.7, bf16[27,96,96]{2,1,0:T(8,128)(2,1)} %param.141, f32[12,8,8,8,96]{4,0,3,2,1:T(8,128)} %fusion.281, ...), kind=kOutput, calls=%fused_computation.88 | convolution fusion | flops 132120576 | bytes 116736000 | tf_op jit(solution)/shard_map/oi,bixyz->boxyz/dot_general | solution.py:65
  302.5 2.8 copy.349
  305.3 55.4 %all_to_all.10 = bf16[8,192,512]{2,1,0:T(8,128)(2,1)S(1)} all-to-all(bf16[8,192,512]{2,1,0:T(8,128)(2,1)} %copy.349), channel_id=1, replica_groups=mesh['gx'=4,'yz'=8] {'yz'}, dimensions={0} | all-to-all | bytes 3145728 | tf_op jit(solution)/shard_map/all_to_all | solution.py:181
  360.7 3.2 fusion.10
  363.9 4.3 all-to-all-start.1
  368.2 4.2 copy.395
  372.4 16.8 %all-to-all-done.1 = bf16[8,192,512]{2,1,0:T(8,128)(2,1)} async-done(((bf16[8,192,512]{2,1,0:T(8,128)(2,1)}), bf16[8,192,512]{2,1,0:T(8,128)(2,1)}, u32[]{:S(2)}, u32[]{:S(2)}) %all-to-all-start.1) | async-done | bytes 1572896 | tf_op jit(solution)/shard_map/all_to_all | solution.py:184
  389.2 3.2 copy.350
  392.4 3.5 copy.351
  396.0 3.6 reshape.2536
  407.3 2.9 gather_fusion.29
  413.1 5.9 collective-permute-start.4
  418.9 3.0 fusion.72
  460.1 3.0 pad_maximum_fusion.3
  464.4 4.5 collective-permute-start.6
  468.9 69.4 %all-reduce.7.cloned.1.call-done = (f32[27,96,96]{2,1,0:T(8,128)}, f32[8,192,96]{1,0,2:T(8,128)}) async-done(((f32[27,96,96]{2,1,0:T(8,128)}, f32[8,192,96]{1,0,2:T(8,128)}), (f32[27,96,96]{2,1,0:T(8,128)}, f32[8,192,96]{1,0,2:T(8,128)})) %all-reduce.7.cloned.1.call-update) | async-done | bytes 1585168 | tf_op jit(solution)/shard_map/psum | solution.py:205
  538.3 90.7 %all-reduce.9.cloned.1.call-done = (f32[27,96,96]{2,1,0:T(8,128)}, f32[8,192,96]{1,0,2:T(8,128)}) async-done(((f32[27,96,96]{2,1,0:T(8,128)}, f32[8,192,96]{1,0,2:T(8,128)}), (f32[27,96,96]{2,1,0:T(8,128)}, f32[8,192,96]{1,0,2:T(8,128)})) %all-reduce.9.cloned.1.call-update) | async-done | bytes 1585168 | tf_op jit(solution)/shard_map/psum | solution.py:205
  631.4 6.2 pad_maximum_fusion.1
  637.7 12.1 %copy.460 = bf16[3,3,8,96,512]{3,2,1,0,4:T(8,128)(2,1)} copy(bf16[3,3,8,96,512]{4,3,2,1,0:T(8,128)(2,1)} %pad_maximum_fusion.1) | data formatting | bytes 14155776 | tf_op jit(solution)/shard_map/concatenate | solution.py:140
  649.7 8.6 %maximum_maximum_fusion.1 = bf16[85,96,8,8,8]{1,0,4,3,2:T(8,128)(2,1)S(1)} fusion(bf16[72,96,8,8,8]{1,0,4,3,2:T(8,128)(2,1)} %bitcast.1017, bf16[12,96,8,8,8]{1,0,4,3,2:T(8,128)(2,1)S(1)} %multiply_convert_fusion, bf16[85]{0:T(256)(128)(2,1)S(1)} %copy-done.95), kind=kLoop, calls=%fused_computation.58 | loop fusion | flops 25067520 | bytes 16613546 | tf_op jit(solution)/shard_map/concatenate | solution.py:140
  664.4 6.3 copy.375
  696.2 5.1 gather_fusion.43
  701.4 2.8 copy.381
  706.2 2.8 copy.369
  717.3 3.1 fusion.279
  720.4 2.7 fusion.283
  723.1 2.8 fusion.287
  733.9 2.8 fusion.303
  739.3 3.0 fusion.311
  745.1 2.8 fusion.319
  750.5 2.7 fusion.327
  755.9 2.8 fusion.335
  761.3 2.7 fusion.343
  766.7 2.8 fusion.351
  772.2 2.7 fusion.359
  777.6 2.8 fusion.367
  788.5 35.2 %fusion.1 = bf16[12,96,8,8,8]{1,0,4,3,2:T(8,128)(2,1)S(1)} fusion(f32[12,8,8,8,96]{4,0,3,2,1:T(8,128)} %fusion.279, f32[12,8,8,8,96]{4,0,3,2,1:T(8,128)} %fusion.283, f32[12,8,8,8,96]{4,0,3,2,1:T(8,128)} %fusion.287, f32[12,8,8,8,96]{4,0,3,2,1:T(8,128)} %fusion.291, f32[12,8,8,8,96]{4,0,3,2,1:T(8,128)} %fusion.295, f32[12,8,8,8,96]{4,0,3,2,1:T(8,128)} %fusion.299, ...), kind=kOutput, calls=%fused_computation.66 | convolution fusion | flops 129761280 | bytes 114376704 | tf_op jit(solution)/shard_map/oi,boxyz->bixyz/dot_general | solution.py:83
  (506 shorter events, 284.3 us)
Async XLA Ops:
  7.2 289.4 %copy-start = (bf16[8,192,96]{2,1,0:T(8,128)(2,1)S(1)}, bf16[8,192,96]{2,1,0:T(8,128)(2,1)}, u32[]{:S(2)}) copy-start(bf16[8,192,96]{2,1,0:T(8,128)(2,1)} %param.142) | copy-start | bytes 884740
  7.2 12.8 %copy-start.11 = (s32[12,27]{1,0:T(8,128)S(1)}, s32[12,27]{1,0:T(8,128)}, u32[]{:S(2)}) copy-start(s32[12,27]{1,0:T(8,128)} %param.137) | copy-start | bytes 3892
  7.2 13.6 %copy-start.93 = (s32[12,2]{0,1:T(2,128)S(1)}, s32[12,2]{0,1:T(2,128)}, u32[]{:S(2)}) copy-start(s32[12,2]{0,1:T(2,128)} %param.139) | copy-start | bytes 292
  7.2 15.0 %copy-start.5 = (s32[4]{0:T(128)S(1)}, s32[4]{0:T(128)}, u32[]{:S(2)}) copy-start(s32[4]{0:T(128)} %param.140) | copy-start | bytes 52
  7.9 33.5 %copy-start.96 = (pred[8]{0:T(512)(128)(4,1)}, pred[8]{0:T(512)(128)(4,1)S(1)}, u32[]{:S(2)}) copy-start(pred[8]{0:T(512)(128)(4,1)S(1)} %compare_and_fusion.27) | copy-start | bytes 28
  8.6 32.8 %copy-start.31 = (s32[1024]{0:T(1024)}, s32[1024]{0:T(1024)S(1)}, u32[]{:S(2)}) copy-start(s32[1024]{0:T(1024)S(1)} %pad_clamp_fusion.28) | copy-start | bytes 12292
  11.4 30.0 %copy-start.8 = (bf16[12,96,512]{2,1,0:T(8,128)(2,1)}, bf16[12,96,512]{2,1,0:T(8,128)(2,1)S(1)}, u32[]{:S(2)}) copy-start(bf16[12,96,512]{2,1,0:T(8,128)(2,1)S(1)} %broadcast_multiply_fusion) | copy-start | bytes 3538948
  12.2 26.1 %collective-permute-start.1 = (bf16[1,1,8,96,512]{4,3,2,1,0:T(8,128)(2,1)S(1)}, bf16[1,1,8,96,512]{4,3,2,1,0:T(8,128)(2,1)S(1)}, u32[]{:S(2)}, u32[]{:S(2)}) collective-permute-start(bf16[1,1,8,96,512]{4,3,2,1,0:T(8,128)(2,1)S(1)} %select_bitcast_fusion.1), channel_id=1, source_target_pairs={{8,0},{16,8},{24,16},{9,1},{17,9},{25,17},{10,2},{18,10},{26,18},{... | collective-permute-start | bytes 2359304 | tf_op jit(solution)/shard_map/ppermute | solution.py:18
  13.5 24.8 %collective-permute-start = (bf16[1,1,8,96,512]{4,3,2,1,0:T(8,128)(2,1)S(1)}, bf16[1,1,8,96,512]{4,3,2,1,0:T(8,128)(2,1)}, u32[]{:S(2)}, u32[]{:S(2)}) collective-permute-start(bf16[1,1,8,96,512]{4,3,2,1,0:T(8,128)(2,1)S(1)} %select_bitcast_fusion.1), channel_id=1, source_target_pairs={{0,8},{8,16},{16,24},{1,9},{9,17},{17,25},{2,10},{10,18},{18,26},{... | collective-permute-start | bytes 2359304 | tf_op jit(solution)/shard_map/ppermute | solution.py:17
  20.3 26.9 %copy-start.50 = (s32[12]{0:T(128)}, s32[12]{0:T(128)S(1)}, u32[]{:S(2)}) copy-start(s32[12]{0:T(128)S(1)} %get-tuple-element.700) | copy-start | bytes 148
  20.3 26.9 %copy-start.68 = (s32[12]{0:T(128)}, s32[12]{0:T(128)S(1)}, u32[]{:S(2)}) copy-start(s32[12]{0:T(128)S(1)} %get-tuple-element.699) | copy-start | bytes 148
  20.8 9.2 %copy-start.63 = (s32[12]{0:T(128)}, s32[12]{0:T(128)S(1)}, u32[]{:S(2)}) copy-start(s32[12]{0:T(128)S(1)} %get-tuple-element.687) | copy-start | bytes 148
  20.8 9.8 %copy-start.62 = (s32[12]{0:T(128)}, s32[12]{0:T(128)S(1)}, u32[]{:S(2)}) copy-start(s32[12]{0:T(128)S(1)} %get-tuple-element.686) | copy-start | bytes 148
  20.8 26.3 %copy-start.51 = (s32[12]{0:T(128)}, s32[12]{0:T(128)S(1)}, u32[]{:S(2)}) copy-start(s32[12]{0:T(128)S(1)} %get-tuple-element.698) | copy-start | bytes 148
  20.9 26.3 %copy-start.52 = (s32[12]{0:T(128)}, s32[12]{0:T(128)S(1)}, u32[]{:S(2)}) copy-start(s32[12]{0:T(128)S(1)} %get-tuple-element.696) | copy-start | bytes 148
  20.9 26.3 %copy-start.53 = (s32[12]{0:T(128)}, s32[12]{0:T(128)S(1)}, u32[]{:S(2)}) copy-start(s32[12]{0:T(128)S(1)} %get-tuple-element.697) | copy-start | bytes 148
  20.9 26.3 %copy-start.54 = (s32[12]{0:T(128)}, s32[12]{0:T(128)S(1)}, u32[]{:S(2)}) copy-start(s32[12]{0:T(128)S(1)} %get-tuple-element.694) | copy-start | bytes 148
  20.9 26.3 %copy-start.55 = (s32[12]{0:T(128)}, s32[12]{0:T(128)S(1)}, u32[]{:S(2)}) copy-start(s32[12]{0:T(128)S(1)} %get-tuple-element.695) | copy-start | bytes 148
  20.9 26.3 %copy-start.56 = (s32[12]{0:T(128)}, s32[12]{0:T(128)S(1)}, u32[]{:S(2)}) copy-start(s32[12]{0:T(128)S(1)} %get-tuple-element.692) | copy-start | bytes 148
  20.9 26.3 %copy-start.57 = (s32[12]{0:T(128)}, s32[12]{0:T(128)S(1)}, u32[]{:S(2)}) copy-start(s32[12]{0:T(128)S(1)} %get-tuple-element.693) | copy-start | bytes 148
  20.9 26.3 %copy-start.58 = (s32[12]{0:T(128)}, s32[12]{0:T(128)S(1)}, u32[]{:S(2)}) copy-start(s32[12]{0:T(128)S(1)} %get-tuple-element.690) | copy-start | bytes 148
  20.9 26.3 %copy-start.59 = (s32[12]{0:T(128)}, s32[12]{0:T(128)S(1)}, u32[]{:S(2)}) copy-start(s32[12]{0:T(128)S(1)} %get-tuple-element.691) | copy-start | bytes 148
  20.9 26.3 %copy-start.60 = (s32[12]{0:T(128)}, s32[12]{0:T(128)S(1)}, u32[]{:S(2)}) copy-start(s32[12]{0:T(128)S(1)} %get-tuple-element.688) | copy-start | bytes 148
  20.9 26.3 %copy-start.61 = (s32[12]{0:T(128)}, s32[12]{0:T(128)S(1)}, u32[]{:S(2)}) copy-start(s32[12]{0:T(128)S(1)} %get-tuple-element.689) | copy-start | bytes 148
  21.0 26.3 %copy-start.64 = (s32[12]{0:T(128)}, s32[12]{0:T(128)S(1)}, u32[]{:S(2)}) copy-start(s32[12]{0:T(128)S(1)} %get-tuple-element.684) | copy-start | bytes 148
  21.0 26.3 %copy-start.65 = (s32[12]{0:T(128)}, s32[12]{0:T(128)S(1)}, u32[]{:S(2)}) copy-start(s32[12]{0:T(128)S(1)} %get-tuple-element.685) | copy-start | bytes 148
  21.0 26.3 %copy-start.66 = (s32[12]{0:T(128)}, s32[12]{0:T(128)S(1)}, u32[]{:S(2)}) copy-start(s32[12]{0:T(128)S(1)} %get-tuple-element.682) | copy-start | bytes 148
  21.0 26.3 %copy-start.67 = (s32[12]{0:T(128)}, s32[12]{0:T(128)S(1)}, u32[]{:S(2)}) copy-start(s32[12]{0:T(128)S(1)} %get-tuple-element.683) | copy-start | bytes 148
  21.0 26.3 %copy-start.69 = (s32[12]{0:T(128)}, s32[12]{0:T(128)S(1)}, u32[]{:S(2)}) copy-start(s32[12]{0:T(128)S(1)} %get-tuple-element.681) | copy-start | bytes 148
  25.2 87.7 %copy-start.27 = (s32[1024]{0:T(1024)}, s32[1024]{0:T(1024)S(1)}, u32[]{:S(2)}) copy-start(s32[1024]{0:T(1024)S(1)} %pad_clamp_fusion.27) | copy-start | bytes 12292
  30.0 88.1 %copy-start.28 = (s32[1024]{0:T(1024)}, s32[1024]{0:T(1024)S(1)}, u32[]{:S(2)}) copy-start(s32[1024]{0:T(1024)S(1)} %pad_clamp_fusion.9) | copy-start | bytes 12292
  30.0 87.5 %copy-start.29 = (s32[1024]{0:T(1024)}, s32[1024]{0:T(1024)S(1)}, u32[]{:S(2)}) copy-start(s32[1024]{0:T(1024)S(1)} %pad_clamp_fusion.7) | copy-start | bytes 12292
  30.7 86.2 %copy-start.30 = (s32[1024]{0:T(1024)}, s32[1024]{0:T(1024)S(1)}, u32[]{:S(2)}) copy-start(s32[1024]{0:T(1024)S(1)} %pad_clamp_fusion.3) | copy-start | bytes 12292
  41.4 25.0 %collective-permute-start.3 = (bf16[3,1,8,96,512]{4,3,2,1,0:T(8,128)(2,1)}, bf16[3,1,8,96,512]{4,3,2,1,0:T(8,128)(2,1)}, u32[]{:S(2)}, u32[]{:S(2)}) collective-permute-start(bf16[3,1,8,96,512]{4,3,2,1,0:T(8,128)(2,1)} %pad_maximum_fusion.2), channel_id=1, source_target_pairs={{1,0},{2,1},{3,2},{4,3},{5,4},{6,5},{7,6},{9,8},{10,9},{11,10},{12... | collective-permute-start | bytes 7077896 | tf_op jit(solution)/shard_map/ppermute | solution.py:18
  42.7 23.7 %collective-permute-start.2 = (bf16[3,1,8,96,512]{4,3,2,1,0:T(8,128)(2,1)}, bf16[3,1,8,96,512]{4,3,2,1,0:T(8,128)(2,1)}, u32[]{:S(2)}, u32[]{:S(2)}) collective-permute-start(bf16[3,1,8,96,512]{4,3,2,1,0:T(8,128)(2,1)} %pad_maximum_fusion.2), channel_id=1, source_target_pairs={{0,1},{1,2},{2,3},{3,4},{4,5},{5,6},{6,7},{8,9},{9,10},{10,11},{11... | collective-permute-start | bytes 7077896 | tf_op jit(solution)/shard_map/ppermute | solution.py:17
  52.1 350.5 %copy-start.12 = (f32[12,512]{0,1:T(8,128)}, f32[12,512]{0,1:T(8,128)S(1)}, u32[]{:S(2)}) copy-start(f32[12,512]{0,1:T(8,128)S(1)} %copy.457) | copy-start | bytes 73732
  72.7 12.1 %copy-start.94 = (bf16[85]{0:T(256)(128)(2,1)S(1)}, bf16[85]{0:T(256)(128)(2,1)}, u32[]{:S(2)}) copy-start(bf16[85]{0:T(256)(128)(2,1)} %pad.231.clone) | copy-start | bytes 514
  153.3 21.5 %copy-start.86 = (pred[12]{0:T(512)(128)(4,1)S(1)}, pred[12]{0:T(512)(128)(4,1)}, u32[]{:S(2)}) copy-start(pred[12]{0:T(512)(128)(4,1)} %get-tuple-element.812) | copy-start | bytes 40
  153.3 22.3 %copy-start.14 = (bf16[12,96,8]{1,2,0:T(8,128)(2,1)S(1)}, bf16[12,96,8]{1,2,0:T(8,128)(2,1)}, u32[]{:S(2)}) copy-start(bf16[12,96,8]{1,2,0:T(8,128)(2,1)} %gather_fusion.17) | copy-start | bytes 55300
  153.3 22.3 %copy-start.45 = (pred[12]{0:T(512)(128)(4,1)S(1)}, pred[12]{0:T(512)(128)(4,1)}, u32[]{:S(2)}) copy-start(pred[12]{0:T(512)(128)(4,1)} %get-tuple-element.811) | copy-start | bytes 40
  153.3 23.0 %copy-start.84 = (pred[12]{0:T(512)(128)(4,1)S(1)}, pred[12]{0:T(512)(128)(4,1)}, u32[]{:S(2)}) copy-start(pred[12]{0:T(512)(128)(4,1)} %get-tuple-element.810) | copy-start | bytes 40
  153.3 23.9 %copy-start.42 = (pred[12]{0:T(512)(128)(4,1)S(1)}, pred[12]{0:T(512)(128)(4,1)}, u32[]{:S(2)}) copy-start(pred[12]{0:T(512)(128)(4,1)} %get-tuple-element.809) | copy-start | bytes 40
  153.4 24.5 %copy-start.77 = (pred[12]{0:T(512)(128)(4,1)S(1)}, pred[12]{0:T(512)(128)(4,1)}, u32[]{:S(2)}) copy-start(pred[12]{0:T(512)(128)(4,1)} %get-tuple-element.808) | copy-start | bytes 40
  153.4 25.2 %copy-start.39 = (pred[12]{0:T(512)(128)(4,1)S(1)}, pred[12]{0:T(512)(128)(4,1)}, u32[]{:S(2)}) copy-start(pred[12]{0:T(512)(128)(4,1)} %get-tuple-element.807) | copy-start | bytes 40
  153.4 25.9 %copy-start.75 = (pred[12]{0:T(512)(128)(4,1)S(1)}, pred[12]{0:T(512)(128)(4,1)}, u32[]{:S(2)}) copy-start(pred[12]{0:T(512)(128)(4,1)} %get-tuple-element.806) | copy-start | bytes 40
  153.4 26.5 %copy-start.36 = (pred[12]{0:T(512)(128)(4,1)S(1)}, pred[12]{0:T(512)(128)(4,1)}, u32[]{:S(2)}) copy-start(pred[12]{0:T(512)(128)(4,1)} %get-tuple-element.805) | copy-start | bytes 40
  153.4 27.3 %copy-start.81 = (pred[12]{0:T(512)(128)(4,1)S(1)}, pred[12]{0:T(512)(128)(4,1)}, u32[]{:S(2)}) copy-start(pred[12]{0:T(512)(128)(4,1)} %get-tuple-element.804) | copy-start | bytes 40
  153.4 28.1 %copy-start.34 = (pred[12]{0:T(512)(128)(4,1)S(1)}, pred[12]{0:T(512)(128)(4,1)}, u32[]{:S(2)}) copy-start(pred[12]{0:T(512)(128)(4,1)} %get-tuple-element.803) | copy-start | bytes 40
  153.4 28.8 %copy-start.72 = (pred[12]{0:T(512)(128)(4,1)S(1)}, pred[12]{0:T(512)(128)(4,1)}, u32[]{:S(2)}) copy-start(pred[12]{0:T(512)(128)(4,1)} %get-tuple-element.802) | copy-start | bytes 40
  153.4 29.5 %copy-start.32 = (pred[12]{0:T(512)(128)(4,1)S(1)}, pred[12]{0:T(512)(128)(4,1)}, u32[]{:S(2)}) copy-start(pred[12]{0:T(512)(128)(4,1)} %get-tuple-element.801) | copy-start | bytes 40
  153.4 30.2 %copy-start.70 = (pred[12]{0:T(512)(128)(4,1)S(1)}, pred[12]{0:T(512)(128)(4,1)}, u32[]{:S(2)}) copy-start(pred[12]{0:T(512)(128)(4,1)} %get-tuple-element.800) | copy-start | bytes 40
  153.4 30.8 %copy-start.16 = (bf16[27,96,96]{2,1,0:T(8,128)(2,1)S(1)}, bf16[27,96,96]{2,1,0:T(8,128)(2,1)}, u32[]{:S(2)}) copy-start(bf16[27,96,96]{2,1,0:T(8,128)(2,1)} %param.141) | copy-start | bytes 1492996
  305.3 55.4 %copy-start.21 = (bf16[8,192,512]{2,1,0:T(8,128)(2,1)S(1)}, bf16[8,192,512]{2,1,0:T(8,128)(2,1)}, u32[]{:S(2)}) copy-start(bf16[8,192,512]{2,1,0:T(8,128)(2,1)} %param.143) | copy-start | bytes 4718596
  363.9 25.4 %all-to-all-start.1 = ((bf16[8,192,512]{2,1,0:T(8,128)(2,1)}), bf16[8,192,512]{2,1,0:T(8,128)(2,1)}, u32[]{:S(2)}, u32[]{:S(2)}) async-start(bf16[8,192,512]{2,1,0:T(8,128)(2,1)} %get-tuple-element.764), calls=%async_computation.1 | async-start | bytes 3145728 | tf_op jit(solution)/shard_map/all_to_all | solution.py:184
  368.2 170.1 %all-reduce.7.cloned.1.call-start = ((), (), s32[]{:S(2)}) async-start(), calls=%async_computation.2 | async-start | bytes 4227072 | tf_op jit(solution)/shard_map/psum | solution.py:205
  411.5 10.4 %copy-start.3 = (bf16[12,96,10,10,10]{1,0,4,3,2:T(8,128)(2,1)S(1)}, bf16[12,96,10,10,10]{1,0,4,3,2:T(8,128)(2,1)}, u32[]{:S(2)}) copy-start(bf16[12,96,10,10,10]{1,0,4,3,2:T(8,128)(2,1)} %constant_dynamic-update-slice_fusion.7) | copy-start | bytes 6912004
  411.5 48.6 %collective-permute-start.5 = (bf16[1,1,8,96,512]{4,3,2,1,0:T(8,128)(2,1)S(1)}, bf16[1,1,8,96,512]{4,3,2,1,0:T(8,128)(2,1)}, u32[]{:S(2)}, u32[]{:S(2)}) collective-permute-start(bf16[1,1,8,96,512]{4,3,2,1,0:T(8,128)(2,1)S(1)} %select_bitcast_fusion), channel_id=1, source_target_pairs={{8,0},{16,8},{24,16},{9,1},{17,9},{25,17},{10,2},{18,10},{26,18},{... | collective-permute-start | bytes 2359304 | tf_op jit(solution)/shard_map/ppermute | solution.py:18
  413.1 47.0 %collective-permute-start.4 = (bf16[1,1,8,96,512]{4,3,2,1,0:T(8,128)(2,1)S(1)}, bf16[1,1,8,96,512]{4,3,2,1,0:T(8,128)(2,1)}, u32[]{:S(2)}, u32[]{:S(2)}) collective-permute-start(bf16[1,1,8,96,512]{4,3,2,1,0:T(8,128)(2,1)S(1)} %select_bitcast_fusion), channel_id=1, source_target_pairs={{0,8},{8,16},{16,24},{1,9},{9,17},{17,25},{2,10},{10,18},{18,26},{... | collective-permute-start | bytes 2359304 | tf_op jit(solution)/shard_map/ppermute | solution.py:17
  460.0 169.1 %all-reduce.9.cloned.1.call-start = ((), (), s32[]{:S(2)}) async-start(), calls=%async_computation.3 | async-start | bytes 4227072 | tf_op jit(solution)/shard_map/psum | solution.py:205
  463.1 168.3 %collective-permute-start.7 = (bf16[3,1,8,96,512]{4,3,2,1,0:T(8,128)(2,1)}, bf16[3,1,8,96,512]{4,3,2,1,0:T(8,128)(2,1)}, u32[]{:S(2)}, u32[]{:S(2)}) collective-permute-start(bf16[3,1,8,96,512]{4,3,2,1,0:T(8,128)(2,1)} %pad_maximum_fusion.3), channel_id=1, source_target_pairs={{1,0},{2,1},{3,2},{4,3},{5,4},{6,5},{7,6},{9,8},{10,9},{11,10},{12... | collective-permute-start | bytes 7077896 | tf_op jit(solution)/shard_map/ppermute | solution.py:18
  464.4 167.0 %collective-permute-start.6 = (bf16[3,1,8,96,512]{4,3,2,1,0:T(8,128)(2,1)}, bf16[3,1,8,96,512]{4,3,2,1,0:T(8,128)(2,1)}, u32[]{:S(2)}, u32[]{:S(2)}) collective-permute-start(bf16[3,1,8,96,512]{4,3,2,1,0:T(8,128)(2,1)} %pad_maximum_fusion.3), channel_id=1, source_target_pairs={{0,1},{1,2},{2,3},{3,4},{4,5},{5,6},{6,7},{8,9},{9,10},{10,11},{11... | collective-permute-start | bytes 7077896 | tf_op jit(solution)/shard_map/ppermute | solution.py:17
  637.6 12.1 %copy-start.95 = (bf16[85]{0:T(256)(128)(2,1)S(1)}, bf16[85]{0:T(256)(128)(2,1)}, u32[]{:S(2)}) copy-start(bf16[85]{0:T(256)(128)(2,1)} %pad.231.clone) | copy-start | bytes 514
  717.3 68.5 %copy-start.4 = (bf16[12,96,10,10,10]{1,0,4,3,2:T(8,128)(2,1)}, bf16[12,96,10,10,10]{1,0,4,3,2:T(8,128)(2,1)S(1)}, u32[]{:S(2)}) copy-start(bf16[12,96,10,10,10]{1,0,4,3,2:T(8,128)(2,1)S(1)} %constant_dynamic-update-slice_fusion) | copy-start | bytes 6912004
  788.5 40.2 %copy-start.1 = (bf16[8,192,96]{2,1,0:T(8,128)(2,1)S(1)}, bf16[8,192,96]{2,1,0:T(8,128)(2,1)}, u32[]{:S(2)}) copy-start(bf16[8,192,96]{2,1,0:T(8,128)(2,1)} %param.142) | copy-start | bytes 884740
  (47 other events, 197.5 us)
Sparse Core Ops, SparseCore 0:
  460.1 78.1 all-reduce.6
  540.8 88.2 all-reduce.8
